TPU v7x, 32 devices: a whole 2x2x4 slice. The times are simulated.
32 devices in a mesh: grp: 1, dap: 32 (over z, y, x, core), sub: 1.
Axes of the slice: x: 2, y: 2, z: 4, core: 2. Of those that a mesh axis runs over, the one named last changes fastest.
Arguments:
- pair: bfloat16 [128, 128, 128], P(('grp', 'dap'), 'sub'), may hold values from -6 to 6
- pair_mask: int32 [128, 128], P(('grp', 'dap'), 'sub'), may hold values 0 or 1
- ln_gain: float32 [128], replicated, may hold values from 0.1 to 1.9
- ln_bias: float32 [128], replicated, may hold values from -3 to 3
- w_proj: bfloat16 [128, 512], replicated, may hold values from -0.5 to 0.5
- w_gate: bfloat16 [128, 128], replicated, may hold values from -0.5 to 0.5
- tri_gain: float32 [128], replicated, may hold values from 0.1 to 1.9
- tri_bias: float32 [128], replicated, may hold values from -3 to 3
- w_out: bfloat16 [128, 128], replicated, may hold values from -0.5 to 0.5
Outputs:
- update: bfloat16 [128, 128, 128], P(('grp', 'dap'), 'sub')
All inputs are finite; a program needn't handle non-finite values. No bound on the sum of `pair_mask` on one device may be relied on, other than what follows from the above.
Results may differ from a plain program's by a relative error of at most 0.018.
Values may be sent and summed in bfloat16 or wider, within the bound.
A program may use at most 64 MiB of HBM per device.

v0:
```python
import jax
import jax.numpy as jnp
from jax import lax
from jax.sharding import PartitionSpec as P


def layer_norm(values, gain, bias, axis):
    mean = jnp.mean(values, axis=axis, keepdims=True)
    var = jnp.mean((values - mean) ** 2, axis=axis, keepdims=True)
    return (values - mean) * lax.rsqrt(var + 1e-05) * gain + bias


def body(pair, pair_mask, ln_gain, ln_bias, w_proj, w_gate, tri_gain, tri_bias, w_out):
    hidden = w_out.shape[0]
    normed = layer_norm(pair.astype(jnp.float32), ln_gain, ln_bias, -1).astype(jnp.bfloat16)
    proj = jnp.einsum("rkc,cd->drk", normed, w_proj, preferred_element_type=jnp.float32)
    maskf = pair_mask.astype(jnp.float32)
    left = (jax.nn.sigmoid(proj[0:hidden]) * proj[hidden : 2 * hidden] * maskf).astype(jnp.bfloat16)
    right = (
        jax.nn.sigmoid(proj[2 * hidden : 3 * hidden]) * proj[3 * hidden : 4 * hidden] * maskf
    ).astype(jnp.bfloat16)
    left_all, right_all = (
        lax.all_to_all(left, "dap", split_axis=0, concat_axis=1, tiled=True),
        lax.all_to_all(right, "dap", split_axis=0, concat_axis=1, tiled=True),
    )
    out_gate = jax.nn.sigmoid(
        jnp.einsum("rjc,cd->rjd", normed, w_gate, preferred_element_type=jnp.float32)
    )
    partial_value = jnp.einsum(
        "hjk,hik->hij", right_all, left_all, preferred_element_type=jnp.float32
    ).astype(jnp.bfloat16)
    moved = lax.all_to_all(partial_value, "dap", split_axis=1, concat_axis=0, tiled=True)
    tri = lax.psum_scatter(
        moved.astype(jnp.float32).astype(jnp.bfloat16), "sub", scatter_dimension=2, tiled=True
    )
    tri_normed = layer_norm(
        tri.astype(jnp.float32), tri_gain[:, None, None], tri_bias[:, None, None], 0
    ).astype(jnp.bfloat16)
    linear = jnp.einsum("crj,cd->rjd", tri_normed, w_out, preferred_element_type=jnp.float32)
    return (out_gate * linear).astype(jnp.bfloat16)


def solution(mesh):
    placed = (
        P(("grp", "dap"), "sub", None),
        P(("grp", "dap"), "sub"),
        P(),
        P(),
        P(),
        P(),
        P(),
        P(),
        P(),
    )
    return jax.shard_map(
        body, mesh=mesh, in_specs=placed, out_specs=P(("grp", "dap"), "sub", None), check_vma=False
    )
```

profile of v0, /device:TPU:0, one launch (start us, length us, event | category | flops | bytes accessed | tf_op | source)
XLA Modules:
  0.0 44.4 jit_solution(10137485666391504935)
XLA Ops:
  0.0 0.0 copy-start
  0.0 0.0 copy-start.1
  0.0 1.1 %convert_reduce_fusion = f32[4,128]{1,0:T(4,128)S(1)} fusion(bf16[4,128,128]{2,1,0:T(8,128)(2,1)} %param.9), kind=kLoop, calls=%fused_computation.9 | loop fusion | flops 130560 | bytes 133120 | tf_op jit(solution)/shard_map/reduce_sum | solution.py:8
  1.1 0.0 copy-done.1
  1.1 0.2 fusion.6
  1.4 0.0 copy-start.3
  1.4 0.7 %copy-done.3 = s32[4,128]{1,0:T(4,128)S(1)} copy-done((s32[4,128]{1,0:T(4,128)S(1)}, s32[4,128]{1,0:T(4,128)}, u32[]{:S(2)}) %copy-start.3) | copy-done | bytes 2072
  2.0 0.0 copy-start.4
  2.0 0.0 copy-start.5
  2.1 0.0 copy-done
  2.1 0.6 %copy-done.4 = f32[128]{0:T(128)S(1)} copy-done((f32[128]{0:T(128)S(1)}, f32[128]{0:T(128)}, u32[]{:S(2)}) %copy-start.4) | copy-done | bytes 536
  2.7 0.0 copy-done.5
  2.7 0.4 convolution_bitcast_fusion
  3.1 0.2 fusion.11
  3.2 0.8 %copy.19 = bf16[128,4,128]{2,1,0:T(4,128)(2,1)} copy(bf16[128,4,128]{0,2,1:T(8,128)(2,1)S(1)} %get-tuple-element.6) | data formatting | bytes 262144 | tf_op jit(solution)/shard_map/convert_element_type | solution.py:18
  4.0 7.3 %all-to-all-start = ((bf16[128,4,128]{2,1,0:T(4,128)(2,1)}), bf16[128,4,128]{2,1,0:T(4,128)(2,1)S(1)}, u32[]{:S(2)}, u32[]{:S(2)}) async-start(bf16[128,4,128]{2,1,0:T(4,128)(2,1)} %copy.19), calls=%async_computation | async-start | bytes 262144 | tf_op jit(solution)/shard_map/all_to_all | solution.py:23
  11.3 0.8 %copy.22 = bf16[128,4,128]{2,1,0:T(4,128)(2,1)} copy(bf16[128,4,128]{0,2,1:T(8,128)(2,1)S(1)} %get-tuple-element.5) | data formatting | bytes 262144 | tf_op jit(solution)/shard_map/convert_element_type | solution.py:21
  12.1 7.4 %all-to-all-done = bf16[128,4,128]{2,1,0:T(4,128)(2,1)S(1)} async-done(((bf16[128,4,128]{2,1,0:T(4,128)(2,1)}), bf16[128,4,128]{2,1,0:T(4,128)(2,1)S(1)}, u32[]{:S(2)}, u32[]{:S(2)}) %all-to-all-start) | async-done | bytes 131104 | tf_op jit(solution)/shard_map/all_to_all | solution.py:23
  19.6 2.6 %all-to-all-start.1 = ((bf16[128,4,128]{2,1,0:T(4,128)(2,1)}), bf16[128,4,128]{2,1,0:T(4,128)(2,1)S(1)}, u32[]{:S(2)}, u32[]{:S(2)}) async-start(bf16[128,4,128]{2,1,0:T(4,128)(2,1)} %copy.22), calls=%async_computation.1 | async-start | bytes 262144 | tf_op jit(solution)/shard_map/all_to_all | solution.py:24
  22.2 0.1 copy.21
  22.3 8.1 %all-to-all-done.1 = bf16[128,4,128]{2,1,0:T(4,128)(2,1)S(1)} async-done(((bf16[128,4,128]{2,1,0:T(4,128)(2,1)}), bf16[128,4,128]{2,1,0:T(4,128)(2,1)S(1)}, u32[]{:S(2)}, u32[]{:S(2)}) %all-to-all-start.1) | async-done | bytes 131104 | tf_op jit(solution)/shard_map/all_to_all | solution.py:24
  30.4 0.1 copy.24
  30.5 0.2 convolution_convert_fusion
  30.7 0.8 %copy.25 = bf16[4,128,128]{2,0,1:T(4,128)(2,1)} copy(bf16[4,128,128]{2,1,0:T(8,128)(2,1)S(1)} %convolution_convert_fusion) | data formatting | bytes 262144 | tf_op jit(solution)/shard_map/convert_element_type | solution.py:31
  31.5 0.0 copy-start.8
  31.5 2.7 %all-to-all-start.2 = ((bf16[4,128,128]{2,0,1:T(4,128)(2,1)}), bf16[4,128,128]{2,0,1:T(4,128)(2,1)S(1)}, u32[]{:S(2)}, u32[]{:S(2)}) async-start(bf16[4,128,128]{2,0,1:T(4,128)(2,1)} %copy.25), calls=%async_computation.2 | async-start | bytes 262144 | tf_op jit(solution)/shard_map/all_to_all | solution.py:32
  34.2 0.0 copy-done.8
  34.2 0.3 fusion.2
  34.6 7.9 %all-to-all-done.2 = bf16[4,128,128]{2,0,1:T(4,128)(2,1)S(1)} async-done(((bf16[4,128,128]{2,0,1:T(4,128)(2,1)}), bf16[4,128,128]{2,0,1:T(4,128)(2,1)S(1)}, u32[]{:S(2)}, u32[]{:S(2)}) %all-to-all-start.2) | async-done | bytes 131104 | tf_op jit(solution)/shard_map/all_to_all | solution.py:32
  42.5 0.1 bitcast_reduce_fusion
  42.5 0.1 fusion.21
  42.6 0.0 copy-start.2
  42.7 0.0 copy-start.6
  42.7 0.0 copy-start.7
  42.7 0.7 %copy-done.2 = bf16[128,128]{1,0:T(8,128)(2,1)S(1)} copy-done((bf16[128,128]{1,0:T(8,128)(2,1)S(1)}, bf16[128,128]{1,0:T(8,128)(2,1)}, u32[]{:S(2)}) %copy-start.2) | copy-done | bytes 32792
  43.4 0.0 copy-done.6
  43.4 0.0 copy-done.7
  43.4 1.0 %fusion.3 = bf16[4,128,128]{2,1,0:T(8,128)(2,1)} fusion(f32[4,128,128]{2,1,0:T(8,128)S(1)} %fusion.2, f32[128,4,128]{2,0,1:T(8,128)S(1)} %bitcast.34, f32[128]{0:T(128)S(1)} %copy-done.6, f32[128]{0:T(128)S(1)} %copy-done.7, f32[4,128]{1,0:T(4,128)S(1)} %add_rsqrt_fusion, f32[4,128]{1,0:T(4,128)S(1)} %broadcast_multiply_fusion, ...), kind=kOutput, calls=%fused_computation.6 | convolution fusion | flops 17235968 | bytes 693248 | tf_op jit(solution)/shard_map/crj,cd->rjd/dot_general | solution.py:39
  (9 shorter events, 0.1 us)
Async XLA Ops:
  0.0 2.1 %copy-start = (bf16[128,512]{1,0:T(8,128)(2,1)S(1)}, bf16[128,512]{1,0:T(8,128)(2,1)}, u32[]{:S(2)}) copy-start(bf16[128,512]{1,0:T(8,128)(2,1)} %param.13) | copy-start | bytes 393220
  0.0 1.1 %copy-start.1 = (bf16[4,128,128]{2,1,0:T(8,128)(2,1)S(1)}, bf16[4,128,128]{2,1,0:T(8,128)(2,1)}, u32[]{:S(2)}) copy-start(bf16[4,128,128]{2,1,0:T(8,128)(2,1)} %param.9) | copy-start | bytes 393220
  1.4 0.7 %copy-start.3 = (s32[4,128]{1,0:T(4,128)S(1)}, s32[4,128]{1,0:T(4,128)}, u32[]{:S(2)}) copy-start(s32[4,128]{1,0:T(4,128)} %param.10) | copy-start | bytes 6148
  2.0 0.7 %copy-start.4 = (f32[128]{0:T(128)S(1)}, f32[128]{0:T(128)}, u32[]{:S(2)}) copy-start(f32[128]{0:T(128)} %param.12) | copy-start | bytes 1540
  2.0 0.7 %copy-start.5 = (f32[128]{0:T(128)S(1)}, f32[128]{0:T(128)}, u32[]{:S(2)}) copy-start(f32[128]{0:T(128)} %param.11) | copy-start | bytes 1540
  4.0 15.5 %all-to-all-start = ((bf16[128,4,128]{2,1,0:T(4,128)(2,1)}), bf16[128,4,128]{2,1,0:T(4,128)(2,1)S(1)}, u32[]{:S(2)}, u32[]{:S(2)}) async-start(bf16[128,4,128]{2,1,0:T(4,128)(2,1)} %copy.19), calls=%async_computation | async-start | bytes 262144 | tf_op jit(solution)/shard_map/all_to_all | solution.py:23
  19.6 10.8 %all-to-all-start.1 = ((bf16[128,4,128]{2,1,0:T(4,128)(2,1)}), bf16[128,4,128]{2,1,0:T(4,128)(2,1)S(1)}, u32[]{:S(2)}, u32[]{:S(2)}) async-start(bf16[128,4,128]{2,1,0:T(4,128)(2,1)} %copy.22), calls=%async_computation.1 | async-start | bytes 262144 | tf_op jit(solution)/shard_map/all_to_all | solution.py:24
  31.5 2.7 %copy-start.8 = (bf16[128,128]{1,0:T(8,128)(2,1)S(1)}, bf16[128,128]{1,0:T(8,128)(2,1)}, u32[]{:S(2)}) copy-start(bf16[128,128]{1,0:T(8,128)(2,1)} %param.14) | copy-start | bytes 98308
  31.5 10.9 %all-to-all-start.2 = ((bf16[4,128,128]{2,0,1:T(4,128)(2,1)}), bf16[4,128,128]{2,0,1:T(4,128)(2,1)S(1)}, u32[]{:S(2)}, u32[]{:S(2)}) async-start(bf16[4,128,128]{2,0,1:T(4,128)(2,1)} %copy.25), calls=%async_computation.2 | async-start | bytes 262144 | tf_op jit(solution)/shard_map/all_to_all | solution.py:32
  42.6 0.8 %copy-start.2 = (bf16[128,128]{1,0:T(8,128)(2,1)S(1)}, bf16[128,128]{1,0:T(8,128)(2,1)}, u32[]{:S(2)}) copy-start(bf16[128,128]{1,0:T(8,128)(2,1)} %param.17) | copy-start | bytes 98308
  42.7 0.7 %copy-start.6 = (f32[128]{0:T(128)S(1)}, f32[128]{0:T(128)}, u32[]{:S(2)}) copy-start(f32[128]{0:T(128)} %param.16) | copy-start | bytes 1540
  42.7 0.7 %copy-start.7 = (f32[128]{0:T(128)S(1)}, f32[128]{0:T(128)}, u32[]{:S(2)}) copy-start(f32[128]{0:T(128)} %param.15) | copy-start | bytes 1540
where the time goes:
time: 44.8 us; the launch traced here: 44.4 us
  waiting for transfers between devices  23.4 us (52%)
  starting transfers between devices  12.6 us (28%)
  local copies, waits for them, and re-layouts  4.66 us (10%)
  matrix products  1.85 us (4%)
  other arithmetic  1.68 us (4%)
    all_to_all x1, waiting for transfers between devices, body(): lax.all_to_all(right, 'dap', split_axis=0, concat_axis=1, tiled=True)  8.09 us
    all_to_all x1, waiting for transfers between devices, body(): lax.all_to_all(partial_value, 'dap', split_axis=1, concat_axis=0, tiled=T...  7.88 us
    all_to_all x1, waiting for transfers between devices, body(): lax.all_to_all(left, 'dap', split_axis=0, concat_axis=1, tiled=True)  7.44 us
    all_to_all x1, starting transfers between devices, body(): lax.all_to_all(left, 'dap', split_axis=0, concat_axis=1, tiled=True)  7.3 us
    all_to_all x1, starting transfers between devices, body(): lax.all_to_all(partial_value, 'dap', split_axis=1, concat_axis=0, tiled=T...  2.71 us
    all_to_all x1, starting transfers between devices, body(): lax.all_to_all(right, 'dap', split_axis=0, concat_axis=1, tiled=True)  2.57 us
    unnamed x18, local copies, waits for them, and re-layouts  2.04 us
    reduce_sum x2, other arithmetic, layer_norm(): mean = jnp.mean(values, axis=axis, keepdims=True)  1.14 us
  transfers between devices with their start and end apart: 3, of which 3 were waited for; matrix products, arithmetic and copies ran while one was open for 3% of the time, Pallas kernels for 0%

commit v1 on v0

--- a/solution.py
+++ b/solution.py
@@ -1,7 +1,14 @@
+import functools
+
 import jax
 import jax.numpy as jnp
 from jax import lax
+from jax.experimental import pallas as pl
+from jax.experimental.pallas import tpu as pltpu
 from jax.sharding import PartitionSpec as P
+
+MESH = pl.DeviceIdType.MESH
+GROUP = 4
 
 
 def layer_norm(values, gain, bias, axis):
@@ -40,6 +47,194 @@
     return (out_gate * linear).astype(jnp.bfloat16)
 
 
+def sigmoid(x):
+    return 0.5 * jnp.tanh(0.5 * x) + 0.5
+
+
+def interleave(parts):
+    tiles = [p.reshape(-1, 8, p.shape[-1]) for p in parts]
+    turned = [pltpu.roll(t, GROUP, 1) for t in tiles]
+    low = lax.broadcasted_iota(jnp.int32, tiles[0].shape, 1) < GROUP
+    even = jnp.concatenate(
+        [jnp.where(low, tiles[0], turned[1]), jnp.where(low, tiles[2], turned[3])], axis=1
+    )
+    odd = jnp.concatenate(
+        [jnp.where(low, turned[0], tiles[1]), jnp.where(low, turned[2], tiles[3])], axis=1
+    )
+    return even.astype(jnp.bfloat16), odd.astype(jnp.bfloat16)
+
+
+def nt_dot(a, b):
+    return lax.dot_general(a, b, (((1,), (1,)), ((), ())), preferred_element_type=jnp.float32)
+
+
+def kernel(
+    n, pair_hbm, mask_hbm, vec_refs, w_proj_hbm, w_gate_hbm, w_out_hbm, out_hbm,
+    pair_v, mask_v, vec_v, w_proj_v, w_gate_v, w_out_v, out_v,
+    send1, recv1, send2, recv2, stage, gate_v, col_v, in_sems, out_sem, sems,
+):
+    me = lax.axis_index("dap")
+    rows, k, hidden = pair_v.shape[0], pair_v.shape[1], w_out_v.shape[0]
+    half = n // 2
+
+    def load(src, dst, i):
+        copy = pltpu.make_async_copy(src, dst, in_sems.at[i])
+        copy.start()
+        return copy
+
+    pair_in = load(pair_hbm, pair_v, 0)
+    proj_in = load(w_proj_hbm, w_proj_v, 1)
+    vec_in = [load(r, vec_v.at[pl.ds(i, 1)], 5 + i) for i, r in enumerate(vec_refs)]
+    mask_in = load(mask_hbm, mask_v, 2)
+    gate_in = load(w_gate_hbm, w_gate_v, 3)
+    out_in = load(w_out_hbm, w_out_v, 4)
+
+    barrier = pltpu.get_barrier_semaphore()
+
+    @pl.loop(1, n)
+    def _(s):
+        pl.semaphore_signal(barrier, inc=1, device_id={"dap": lax.rem(me + s, n)}, device_id_type=MESH)
+
+    proj_in.wait()
+    w_t = w_proj_v[...].T
+    pair_in.wait()
+    for copy in vec_in:
+        copy.wait()
+    mask_in.wait()
+    gain, bias = vec_v[0:1, :], vec_v[1:2, :]
+    lefts, rights, normeds = [], [], []
+    for r in range(rows):
+        x = pair_v[r].astype(jnp.float32)
+        centred = x - jnp.mean(x, axis=1, keepdims=True)
+        var = jnp.mean(centred * centred, axis=1, keepdims=True)
+        normed = (centred * lax.rsqrt(var + 1e-05) * gain + bias).astype(jnp.bfloat16)
+        pair_v[r] = normed
+        proj = nt_dot(w_t, normed)
+        mask = mask_v[r : r + 1, :].astype(jnp.float32)
+        lefts.append(sigmoid(proj[0:hidden]) * proj[hidden : 2 * hidden] * mask)
+        rights.append(sigmoid(proj[2 * hidden : 3 * hidden]) * proj[3 * hidden : 4 * hidden] * mask)
+    for side, parts in enumerate((lefts, rights)):
+        even, odd = interleave(parts)
+        send1[:, 0, side] = even
+        send1[:, 1, side] = odd
+
+    def exchange(send, recv, sem):
+        @pl.loop(1, n)
+        def _(s):
+            to = lax.rem(me + s, n)
+            pltpu.make_async_remote_copy(
+                src_ref=send.at[to // 2, lax.rem(to, 2)],
+                dst_ref=recv.at[me],
+                send_sem=sems.at[2 * sem],
+                recv_sem=sems.at[2 * sem + 1],
+                device_id={"dap": to},
+                device_id_type=MESH,
+            ).start()
+
+        recv[me] = send[me // 2, lax.rem(me, 2)]
+
+    def wait_all(recv, i):
+        span = recv.at[pl.ds(0, n - 1)]
+        pltpu.make_async_copy(span, span, sems.at[i]).wait()
+
+    pl.semaphore_wait(barrier, n - 1)
+    exchange(send1, recv1, 0)
+
+    gate_in.wait()
+    for r in range(rows):
+        gate_v[r] = sigmoid(jnp.dot(pair_v[r], w_gate_v[...], preferred_element_type=jnp.float32))
+    for i in range(2):
+        col_v[i] = jnp.broadcast_to(vec_v[2 + i : 3 + i, :], (hidden, hidden)).T
+    out_in.wait()
+
+    wait_all(recv1, 1)
+    for side in range(2):
+        stage[side] = recv1[:, side].astype(jnp.float32).reshape(n * 16, k)
+    products = []
+    for c in range(GROUP):
+        left = stage[0, pl.ds(c, n * rows, stride=GROUP), :].astype(jnp.bfloat16)
+        right = stage[1, pl.ds(c, n * rows, stride=GROUP), :].astype(jnp.bfloat16)
+        products.append(nt_dot(left, right))
+    even, odd = interleave(products)
+    send2[:, 0] = even
+    send2[:, 1] = odd
+    exchange(send2, recv2, 1)
+    wait_all(recv2, 3)
+
+    stage[0] = recv2[...].astype(jnp.float32).reshape(n * 16, k)
+    copies = []
+    for r in range(rows):
+        t = stage[0, pl.ds(r, hidden, stride=GROUP), :]
+        centred = t - jnp.mean(t, axis=0, keepdims=True)
+        var = jnp.mean(centred * centred, axis=0, keepdims=True)
+        normed = (centred * lax.rsqrt(var + 1e-05) * col_v[0] + col_v[1]).astype(jnp.bfloat16)
+        linear = lax.dot_general(
+            normed, w_out_v[...], (((0,), (0,)), ((), ())), preferred_element_type=jnp.float32
+        )
+        out_v[r] = (gate_v[r] * linear).astype(jnp.bfloat16)
+        copy = pltpu.make_async_copy(out_v.at[r], out_hbm.at[r], out_sem.at[r])
+        copy.start()
+        copies.append(copy)
+    wait_all(recv1, 0)
+    wait_all(recv2, 2)
+    for copy in copies:
+        copy.wait()
+
+
+def fused(n, pair, pair_mask, ln_gain, ln_bias, w_proj, w_gate, tri_gain, tri_bias, w_out):
+    rows, k, c = pair.shape
+    hidden = w_out.shape[0]
+    bf16, f32 = jnp.bfloat16, jnp.float32
+    vecs = [v.reshape(1, -1) for v in (ln_gain, ln_bias, tri_gain, tri_bias)]
+    any_spec = pl.BlockSpec(memory_space=pl.ANY)
+
+    def run(pair_r, mask_r, g1, b1, g2, b2, wp, wg, wo, out_r, *scratch):
+        kernel(n, pair_r, mask_r, (g1, b1, g2, b2), wp, wg, wo, out_r, *scratch)
+
+    return pl.pallas_call(
+        run,
+        out_shape=jax.ShapeDtypeStruct((rows, k, c), bf16),
+        in_specs=[any_spec] * 9,
+        out_specs=any_spec,
+        scratch_shapes=[
+            pltpu.VMEM((rows, k, c), bf16),
+            pltpu.VMEM((rows, k), jnp.int32),
+            pltpu.VMEM((8, c), f32),
+            pltpu.VMEM(w_proj.shape, bf16),
+            pltpu.VMEM(w_gate.shape, bf16),
+            pltpu.VMEM(w_out.shape, bf16),
+            pltpu.VMEM((rows, k, c), bf16),
+            pltpu.VMEM((n // 2, 2, 2, 16, k), bf16),
+            pltpu.VMEM((n, 2, 16, k), bf16),
+            pltpu.VMEM((n // 2, 2, 16, k), bf16),
+            pltpu.VMEM((n, 16, k), bf16),
+            pltpu.VMEM((2, n * 16, k), f32),
+            pltpu.VMEM((rows, k, c), f32),
+            pltpu.VMEM((2, hidden, k), f32),
+            pltpu.SemaphoreType.DMA((9,)),
+            pltpu.SemaphoreType.DMA((rows,)),
+            pltpu.SemaphoreType.DMA((4,)),
+        ],
+        compiler_params=pltpu.CompilerParams(
+            collective_id=0, has_side_effects=True, vmem_limit_bytes=16 * 2**20
+        ),
+    )(pair, pair_mask, *vecs, w_proj, w_gate, w_out)
+
+
+def fits(mesh, pair, w_out):
+    n = mesh.shape["dap"]
+    rows, k, c = pair.shape
+    return (
+        mesh.shape["sub"] == 1
+        and n % 4 == 0
+        and rows == GROUP
+        and w_out.shape[0] == GROUP * n
+        and k == rows * n
+        and c == k
+        and k % 128 == 0
+    )
+
+
 def solution(mesh):
     placed = (
         P(("grp", "dap"), "sub", None),
@@ -52,6 +247,12 @@
         P(),
         P(),
     )
+
+    def local(pair, *rest):
+        if fits(mesh, pair, rest[-1]):
+            return fused(mesh.shape["dap"], pair, *rest)
+        return body(pair, *rest)
+
     return jax.shard_map(
-        body, mesh=mesh, in_specs=placed, out_specs=P(("grp", "dap"), "sub", None), check_vma=False
-    )
+        local, mesh=mesh, in_specs=placed, out_specs=P(("grp", "dap"), "sub", None), check_vma=False
+    )

time: 44.8 us -> 26.9 us (0.60)
  waiting for transfers between devices: 23.4 us -> 0 us
  Pallas kernels: 0 us -> 21.9 us
  starting transfers between devices: 12.6 us -> 0 us
  matrix products: 1.85 us -> 0 us
  other arithmetic: 1.68 us -> 0 us
    all_to_all x3 -> x0, waiting for transfers between devices: 23.4 us -> none  [the longest x1 8.09 us: body(): lax.all_to_all(right, 'dap', split_axis=0, concat_axis=1, tiled=True)]
    pallas_call x0 -> x1, Pallas kernels: none -> 21.9 us  [fused(): pl.pallas_call(run, out_shape=jax.ShapeDtypeStruct((rows, k, c), bf16), i...]
    all_to_all x3 -> x0, starting transfers between devices: 12.6 us -> none  [the longest x1 7.3 us: body(): lax.all_to_all(left, 'dap', split_axis=0, concat_axis=1, tiled=True)]
    unnamed x18 -> x19, local copies, waits for them, and re-layouts: 2.04 us -> 4.69 us
    convert_element_type x4 -> x0, local copies, waits for them, and re-layouts: 2.37 us -> none  [the longest x1 0.79 us: body(): (jax.nn.sigmoid(proj[0:hidden]) * proj[hidden:2 * hidden] * maskf).astype...]
    dot_general x4 -> x0, matrix products: 1.85 us -> none  [the longest x1 0.96 us: body(): jnp.einsum('crj,cd->rjd', tri_normed, w_out, preferred_element_type=jnp.f...]
    reduce_sum x4 -> x0, other arithmetic: 1.46 us -> none  [the longest x2 1.14 us: layer_norm(): mean = jnp.mean(values, axis=axis, keepdims=True)]
  transfers between devices with their start and end apart: 3 -> 0, of which waited for: 3 -> 0; matrix products, arithmetic and copies ran while one was open for 3% -> 0% of each run, Pallas kernels for 0% -> 0%
where the time goes in v1:
time: 26.9 us; the launch traced here: 26.6 us
  Pallas kernels  21.9 us (81%)
  local copies, waits for them, and re-layouts  4.69 us (17%)
    pallas_call x1, Pallas kernels, fused(): pl.pallas_call(run, out_shape=jax.ShapeDtypeStruct((rows, k, c), bf16), i...  21.9 us
    unnamed x19, local copies, waits for them, and re-layouts  4.69 us

profile of v1, /device:TPU:0, one launch (start us, length us, event | category | flops | bytes accessed | tf_op | source)
XLA Modules:
  0.0 26.6 jit_solution(10357577595167736339)
XLA Ops:
  0.0 0.0 copy-start.8
  0.0 0.0 copy-start.4
  0.0 0.0 copy-start.5
  0.0 0.0 copy-start.6
  0.0 0.0 copy-start.7
  0.0 0.6 %copy-done.8 = f32[128]{0:T(128)S(1)} copy-done((f32[128]{0:T(128)S(1)}, f32[128]{0:T(128)}, u32[]{:S(2)}) %copy-start.8) | copy-done | bytes 536
  0.7 0.0 copy-done.4
  0.7 0.0 copy-done.5
  0.7 0.0 copy-done.6
  0.7 0.0 copy-done.7
  0.7 0.0 copy-start
  0.7 0.9 %copy-done = bf16[4,128,128]{2,1,0:T(8,128)(2,1)S(1)} copy-done((bf16[4,128,128]{2,1,0:T(8,128)(2,1)S(1)}, bf16[4,128,128]{2,1,0:T(8,128)(2,1)}, u32[]{:S(2)}) %copy-start) | copy-done | bytes 131096
  1.6 0.0 copy-start.1
  1.6 0.9 %copy-done.1 = bf16[128,512]{1,0:T(8,128)(2,1)S(1)} copy-done((bf16[128,512]{1,0:T(8,128)(2,1)S(1)}, bf16[128,512]{1,0:T(8,128)(2,1)}, u32[]{:S(2)}) %copy-start.1) | copy-done | bytes 131096
  2.5 0.0 copy-start.2
  2.5 0.8 %copy-done.2 = bf16[128,128]{1,0:T(8,128)(2,1)S(1)} copy-done((bf16[128,128]{1,0:T(8,128)(2,1)S(1)}, bf16[128,128]{1,0:T(8,128)(2,1)}, u32[]{:S(2)}) %copy-start.2) | copy-done | bytes 32792
  3.3 0.0 copy-start.3
  3.3 0.8 %copy-done.3 = bf16[128,128]{1,0:T(8,128)(2,1)S(1)} copy-done((bf16[128,128]{1,0:T(8,128)(2,1)S(1)}, bf16[128,128]{1,0:T(8,128)(2,1)}, u32[]{:S(2)}) %copy-start.3) | copy-done | bytes 32792
  4.0 21.9 %shard_map.91 = bf16[4,128,128]{2,1,0:T(8,128)(2,1)S(1)} custom-call(bf16[4,128,128]{2,1,0:T(8,128)(2,1)S(1)} %copy-done, s32[4,128]{1,0:T(4,128)S(1)} %copy-done.4, f32[1,128]{1,0:T(1,128)S(1)} %bitcast.4, f32[1,128]{1,0:T(1,128)S(1)} %bitcast.5, f32[1,128]{1,0:T(1,128)S(1)} %bitcast.6, f32[1,128]{1,0:T(1,128)S(1)} %bitcast.7, ...), custom_call_target="tpu_custom_call" | custom-call | tf_op jit(solution)/shard_map/pallas_call | solution.py:194
  25.9 0.7 %copy.11 = bf16[4,128,128]{2,1,0:T(8,128)(2,1)} copy(bf16[4,128,128]{2,1,0:T(8,128)(2,1)S(1)} %shard_map.91) | data formatting | bytes 262144
Async XLA Ops:
  0.0 0.7 %copy-start.8 = (f32[128]{0:T(128)S(1)}, f32[128]{0:T(128)}, u32[]{:S(2)}) copy-start(f32[128]{0:T(128)} %param.16) | copy-start | bytes 1540
  0.0 0.7 %copy-start.4 = (s32[4,128]{1,0:T(4,128)S(1)}, s32[4,128]{1,0:T(4,128)}, u32[]{:S(2)}) copy-start(s32[4,128]{1,0:T(4,128)} %mask_r.1) | copy-start | bytes 6148
  0.0 0.7 %copy-start.5 = (f32[128]{0:T(128)S(1)}, f32[128]{0:T(128)}, u32[]{:S(2)}) copy-start(f32[128]{0:T(128)} %param.11) | copy-start | bytes 1540
  0.0 0.7 %copy-start.6 = (f32[128]{0:T(128)S(1)}, f32[128]{0:T(128)}, u32[]{:S(2)}) copy-start(f32[128]{0:T(128)} %param.12) | copy-start | bytes 1540
  0.0 0.7 %copy-start.7 = (f32[128]{0:T(128)S(1)}, f32[128]{0:T(128)}, u32[]{:S(2)}) copy-start(f32[128]{0:T(128)} %param.15) | copy-start | bytes 1540
  0.7 0.9 %copy-start = (bf16[4,128,128]{2,1,0:T(8,128)(2,1)S(1)}, bf16[4,128,128]{2,1,0:T(8,128)(2,1)}, u32[]{:S(2)}) copy-start(bf16[4,128,128]{2,1,0:T(8,128)(2,1)} %pair_r.1) | copy-start | bytes 393220
  1.6 0.9 %copy-start.1 = (bf16[128,512]{1,0:T(8,128)(2,1)S(1)}, bf16[128,512]{1,0:T(8,128)(2,1)}, u32[]{:S(2)}) copy-start(bf16[128,512]{1,0:T(8,128)(2,1)} %wp.1) | copy-start | bytes 393220
  2.5 0.8 %copy-start.2 = (bf16[128,128]{1,0:T(8,128)(2,1)S(1)}, bf16[128,128]{1,0:T(8,128)(2,1)}, u32[]{:S(2)}) copy-start(bf16[128,128]{1,0:T(8,128)(2,1)} %wg.1) | copy-start | bytes 98308
  3.3 0.8 %copy-start.3 = (bf16[128,128]{1,0:T(8,128)(2,1)S(1)}, bf16[128,128]{1,0:T(8,128)(2,1)}, u32[]{:S(2)}) copy-start(bf16[128,128]{1,0:T(8,128)(2,1)} %wo.1) | copy-start | bytes 98308

commit v2 on v1

--- a/solution.py
+++ b/solution.py
@@ -69,9 +69,9 @@
 
 
 def kernel(
-    n, pair_hbm, mask_hbm, vec_refs, w_proj_hbm, w_gate_hbm, w_out_hbm, out_hbm,
-    pair_v, mask_v, vec_v, w_proj_v, w_gate_v, w_out_v, out_v,
-    send1, recv1, send2, recv2, stage, gate_v, col_v, in_sems, out_sem, sems,
+    n, pair_hbm, mask_hbm, vec_refs, w_proj_hbm, w_gate_hbm, w_out_hbm, out_v,
+    pair_v, mask_v, vec_v, w_proj_v, w_gate_v, w_out_v,
+    send1, recv1, send2, recv2, stage, gate_v, col_v, in_sems, sems,
 ):
     me = lax.axis_index("dap")
     rows, k, hidden = pair_v.shape[0], pair_v.shape[1], w_out_v.shape[0]
@@ -162,7 +162,6 @@
     wait_all(recv2, 3)
 
     stage[0] = recv2[...].astype(jnp.float32).reshape(n * 16, k)
-    copies = []
     for r in range(rows):
         t = stage[0, pl.ds(r, hidden, stride=GROUP), :]
         centred = t - jnp.mean(t, axis=0, keepdims=True)
@@ -172,13 +171,8 @@
             normed, w_out_v[...], (((0,), (0,)), ((), ())), preferred_element_type=jnp.float32
         )
         out_v[r] = (gate_v[r] * linear).astype(jnp.bfloat16)
-        copy = pltpu.make_async_copy(out_v.at[r], out_hbm.at[r], out_sem.at[r])
-        copy.start()
-        copies.append(copy)
     wait_all(recv1, 0)
     wait_all(recv2, 2)
-    for copy in copies:
-        copy.wait()
 
 
 def fused(n, pair, pair_mask, ln_gain, ln_bias, w_proj, w_gate, tri_gain, tri_bias, w_out):
@@ -186,7 +180,7 @@
     hidden = w_out.shape[0]
     bf16, f32 = jnp.bfloat16, jnp.float32
     vecs = [v.reshape(1, -1) for v in (ln_gain, ln_bias, tri_gain, tri_bias)]
-    any_spec = pl.BlockSpec(memory_space=pl.ANY)
+    hbm_spec = pl.BlockSpec(memory_space=pltpu.HBM)
 
     def run(pair_r, mask_r, g1, b1, g2, b2, wp, wg, wo, out_r, *scratch):
         kernel(n, pair_r, mask_r, (g1, b1, g2, b2), wp, wg, wo, out_r, *scratch)
@@ -194,8 +188,8 @@
     return pl.pallas_call(
         run,
         out_shape=jax.ShapeDtypeStruct((rows, k, c), bf16),
-        in_specs=[any_spec] * 9,
-        out_specs=any_spec,
+        in_specs=[hbm_spec] * 9,
+        out_specs=pl.BlockSpec(memory_space=pltpu.VMEM),
         scratch_shapes=[
             pltpu.VMEM((rows, k, c), bf16),
             pltpu.VMEM((rows, k), jnp.int32),
@@ -203,7 +197,6 @@
             pltpu.VMEM(w_proj.shape, bf16),
             pltpu.VMEM(w_gate.shape, bf16),
             pltpu.VMEM(w_out.shape, bf16),
-            pltpu.VMEM((rows, k, c), bf16),
             pltpu.VMEM((n // 2, 2, 2, 16, k), bf16),
             pltpu.VMEM((n, 2, 16, k), bf16),
             pltpu.VMEM((n // 2, 2, 16, k), bf16),
@@ -212,13 +205,12 @@
             pltpu.VMEM((rows, k, c), f32),
             pltpu.VMEM((2, hidden, k), f32),
             pltpu.SemaphoreType.DMA((9,)),
-            pltpu.SemaphoreType.DMA((rows,)),
             pltpu.SemaphoreType.DMA((4,)),
         ],
         compiler_params=pltpu.CompilerParams(
             collective_id=0, has_side_effects=True, vmem_limit_bytes=16 * 2**20
         ),
-    )(pair, pair_mask, *vecs, w_proj, w_gate, w_out)
+    )(*[pltpu.with_memory_space_constraint(x, pltpu.HBM) for x in (pair, pair_mask, *vecs, w_proj, w_gate, w_out)])
 
 
 def fits(mesh, pair, w_out):

time: 26.9 us -> 21.4 us (0.80)
  local copies, waits for them, and re-layouts: 4.69 us -> 0.66 us
  Pallas kernels: 21.9 us -> 20.6 us
    unnamed x19 -> x1, local copies, waits for them, and re-layouts: 4.69 us -> 0.66 us
    pallas_call x1, Pallas kernels: 21.9 us -> 20.6 us  [fused(): pl.pallas_call(run, out_shape=jax.ShapeDtypeStruct((rows, k, c), bf16), i...]
where the time goes in v2:
time: 21.4 us; the launch traced here: 21.2 us
  Pallas kernels  20.6 us (96%)
  local copies, waits for them, and re-layouts  0.66 us (3%)
    pallas_call x1, Pallas kernels, fused(): pl.pallas_call(run, out_shape=jax.ShapeDtypeStruct((rows, k, c), bf16), i...  20.6 us
    unnamed x1, local copies, waits for them, and re-layouts  0.66 us

profile of v2, /device:TPU:0, one launch (start us, length us, event | category | flops | bytes accessed | tf_op | source)
XLA Modules:
  0.0 21.2 jit_solution(3601520832926344262)
XLA Ops:
  0.0 20.6 %shard_map.91 = bf16[4,128,128]{2,1,0:T(8,128)(2,1)S(1)} custom-call(bf16[4,128,128]{2,1,0:T(8,128)(2,1)} %pair_r.1, s32[4,128]{1,0:T(4,128)} %mask_r.1, f32[1,128]{1,0:T(1,128)} %bitcast.4, f32[1,128]{1,0:T(1,128)} %bitcast.5, f32[1,128]{1,0:T(1,128)} %bitcast.6, f32[1,128]{1,0:T(1,128)} %bitcast.7, bf16[128,512]{1,0:T(8,128)(2,1)} %wp.1, ...), custom_call_target="tpu_custom_call" | custom-call | tf_op jit(solution)/shard_map/pallas_call | solution.py:188
  20.6 0.7 %copy.11 = bf16[4,128,128]{2,1,0:T(8,128)(2,1)} copy(bf16[4,128,128]{2,1,0:T(8,128)(2,1)S(1)} %shard_map.91) | data formatting | bytes 262144

commit v3 on v2

--- a/solution.py
+++ b/solution.py
@@ -8,7 +8,7 @@
 from jax.sharding import PartitionSpec as P
 
 MESH = pl.DeviceIdType.MESH
-GROUP = 4
+OWNED = 8
 
 
 def layer_norm(values, gain, bias, axis):
@@ -51,19 +51,6 @@
     return 0.5 * jnp.tanh(0.5 * x) + 0.5
 
 
-def interleave(parts):
-    tiles = [p.reshape(-1, 8, p.shape[-1]) for p in parts]
-    turned = [pltpu.roll(t, GROUP, 1) for t in tiles]
-    low = lax.broadcasted_iota(jnp.int32, tiles[0].shape, 1) < GROUP
-    even = jnp.concatenate(
-        [jnp.where(low, tiles[0], turned[1]), jnp.where(low, tiles[2], turned[3])], axis=1
-    )
-    odd = jnp.concatenate(
-        [jnp.where(low, turned[0], tiles[1]), jnp.where(low, turned[2], tiles[3])], axis=1
-    )
-    return even.astype(jnp.bfloat16), odd.astype(jnp.bfloat16)
-
-
 def nt_dot(a, b):
     return lax.dot_general(a, b, (((1,), (1,)), ((), ())), preferred_element_type=jnp.float32)
 
@@ -71,29 +58,60 @@
 def kernel(
     n, pair_hbm, mask_hbm, vec_refs, w_proj_hbm, w_gate_hbm, w_out_hbm, out_v,
     pair_v, mask_v, vec_v, w_proj_v, w_gate_v, w_out_v,
-    send1, recv1, send2, recv2, stage, gate_v, col_v, in_sems, sems,
+    send_r, recv_r, send_l, recv_l, send_t, recv_t, stage, gate_v, col_v,
+    in_sems, r_sems, l_sems, t_sems,
 ):
     me = lax.axis_index("dap")
     rows, k, hidden = pair_v.shape[0], pair_v.shape[1], w_out_v.shape[0]
     half = n // 2
+    base, place = me // half * half, lax.rem(me, half)
 
     def load(src, dst, i):
         copy = pltpu.make_async_copy(src, dst, in_sems.at[i])
         copy.start()
         return copy
 
+    def each_other(act):
+        @pl.loop(0, half)
+        def _(s):
+            to = lax.rem(place + s, half)
+            act(half - base + to, to)
+
+    def each_own(act):
+        @pl.loop(1, half)
+        def _(s):
+            to = lax.rem(place + s, half)
+            act(base + to, to)
+
+    def greet(to, _):
+        pl.semaphore_signal(barrier, inc=1, device_id={"dap": to}, device_id_type=MESH)
+
+    barrier = pltpu.get_barrier_semaphore()
     pair_in = load(pair_hbm, pair_v, 0)
     proj_in = load(w_proj_hbm, w_proj_v, 1)
+    each_other(greet)
+    each_own(greet)
     vec_in = [load(r, vec_v.at[pl.ds(i, 1)], 5 + i) for i, r in enumerate(vec_refs)]
     mask_in = load(mask_hbm, mask_v, 2)
     gate_in = load(w_gate_hbm, w_gate_v, 3)
     out_in = load(w_out_hbm, w_out_v, 4)
 
-    barrier = pltpu.get_barrier_semaphore()
-
-    @pl.loop(1, n)
-    def _(s):
-        pl.semaphore_signal(barrier, inc=1, device_id={"dap": lax.rem(me + s, n)}, device_id_type=MESH)
+    def sender(send, recv, slot, sems):
+        def act(to, to_place):
+            pltpu.make_async_remote_copy(
+                src_ref=send.at[to_place],
+                dst_ref=recv.at[slot],
+                send_sem=sems.at[0],
+                recv_sem=sems.at[1],
+                device_id={"dap": to},
+                device_id_type=MESH,
+            ).start()
+
+        return act
+
+    def wait_blocks(recv, sem, count):
+        span = recv.at[pl.ds(0, count)]
+        pltpu.make_async_copy(span, span, sem).wait()
 
     proj_in.wait()
     w_t = w_proj_v[...].T
@@ -102,7 +120,11 @@
         copy.wait()
     mask_in.wait()
     gain, bias = vec_v[0:1, :], vec_v[1:2, :]
-    lefts, rights, normeds = [], [], []
+
+    def edge(proj, mask):
+        return sigmoid(proj[0:hidden]) * proj[hidden : 2 * hidden] * mask
+
+    lefts, rights = [], []
     for r in range(rows):
         x = pair_v[r].astype(jnp.float32)
         centred = x - jnp.mean(x, axis=1, keepdims=True)
@@ -111,59 +133,47 @@
         pair_v[r] = normed
         proj = nt_dot(w_t, normed)
         mask = mask_v[r : r + 1, :].astype(jnp.float32)
-        lefts.append(sigmoid(proj[0:hidden]) * proj[hidden : 2 * hidden] * mask)
-        rights.append(sigmoid(proj[2 * hidden : 3 * hidden]) * proj[3 * hidden : 4 * hidden] * mask)
-    for side, parts in enumerate((lefts, rights)):
-        even, odd = interleave(parts)
-        send1[:, 0, side] = even
-        send1[:, 1, side] = odd
-
-    def exchange(send, recv, sem):
-        @pl.loop(1, n)
-        def _(s):
-            to = lax.rem(me + s, n)
-            pltpu.make_async_remote_copy(
-                src_ref=send.at[to // 2, lax.rem(to, 2)],
-                dst_ref=recv.at[me],
-                send_sem=sems.at[2 * sem],
-                recv_sem=sems.at[2 * sem + 1],
-                device_id={"dap": to},
-                device_id_type=MESH,
-            ).start()
-
-        recv[me] = send[me // 2, lax.rem(me, 2)]
-
-    def wait_all(recv, i):
-        span = recv.at[pl.ds(0, n - 1)]
-        pltpu.make_async_copy(span, span, sems.at[i]).wait()
-
+        lefts.append(edge(proj[0 : 2 * hidden], mask).reshape(half, OWNED, k))
+        rights.append(edge(proj[2 * hidden : 4 * hidden], mask).reshape(half, OWNED, k))
+    send_r[...] = jnp.concatenate(rights, axis=1).astype(jnp.bfloat16)
+    send_l[...] = jnp.concatenate(lefts, axis=1).astype(jnp.bfloat16)
     pl.semaphore_wait(barrier, n - 1)
-    exchange(send1, recv1, 0)
+    each_other(sender(send_r, recv_r, me, r_sems))
+    each_own(sender(send_r, recv_r, me, r_sems))
+    each_own(sender(send_l, recv_l, place, l_sems))
+    recv_r[me] = send_r[place]
+    recv_l[place] = send_l[place]
 
     gate_in.wait()
     for r in range(rows):
         gate_v[r] = sigmoid(jnp.dot(pair_v[r], w_gate_v[...], preferred_element_type=jnp.float32))
     for i in range(2):
-        col_v[i] = jnp.broadcast_to(vec_v[2 + i : 3 + i, :], (hidden, hidden)).T
+        col_v[i] = jnp.broadcast_to(vec_v[2 + i : 3 + i, :], (k, hidden)).T
     out_in.wait()
 
-    wait_all(recv1, 1)
-    for side in range(2):
-        stage[side] = recv1[:, side].astype(jnp.float32).reshape(n * 16, k)
+    ours = half * rows
+    wait_blocks(recv_l, l_sems.at[1], half - 1)
+    lefts = []
+    area = stage.at[pl.ds(0, ours * OWNED)]
+    area[...] = recv_l[...].astype(jnp.float32).reshape(ours * OWNED, k)
+    for c in range(OWNED):
+        lefts.append(area[pl.ds(c, ours, stride=OWNED), :].astype(jnp.bfloat16))
+    wait_blocks(recv_r, r_sems.at[1], n - 1)
+    stage[...] = recv_r[...].astype(jnp.float32).reshape(n * rows * OWNED, k)
     products = []
-    for c in range(GROUP):
-        left = stage[0, pl.ds(c, n * rows, stride=GROUP), :].astype(jnp.bfloat16)
-        right = stage[1, pl.ds(c, n * rows, stride=GROUP), :].astype(jnp.bfloat16)
-        products.append(nt_dot(left, right))
-    even, odd = interleave(products)
-    send2[:, 0] = even
-    send2[:, 1] = odd
-    exchange(send2, recv2, 1)
-    wait_all(recv2, 3)
-
-    stage[0] = recv2[...].astype(jnp.float32).reshape(n * 16, k)
+    for c in range(OWNED):
+        right = stage[pl.ds(c, n * rows, stride=OWNED), :].astype(jnp.bfloat16)
+        products.append(nt_dot(lefts[c], right))
+    for c in range(OWNED):
+        area[pl.ds(c, ours, stride=OWNED), :] = products[c]
+    send_t[...] = area[...].astype(jnp.bfloat16).reshape(half, rows * OWNED, k)
+    each_own(sender(send_t, recv_t, place, t_sems))
+    recv_t[place] = send_t[place]
+
+    wait_blocks(recv_t, t_sems.at[1], half - 1)
+    tri = recv_t[...].astype(jnp.float32)
     for r in range(rows):
-        t = stage[0, pl.ds(r, hidden, stride=GROUP), :]
+        t = tri[:, r * OWNED : (r + 1) * OWNED].reshape(hidden, k)
         centred = t - jnp.mean(t, axis=0, keepdims=True)
         var = jnp.mean(centred * centred, axis=0, keepdims=True)
         normed = (centred * lax.rsqrt(var + 1e-05) * col_v[0] + col_v[1]).astype(jnp.bfloat16)
@@ -171,8 +181,9 @@
             normed, w_out_v[...], (((0,), (0,)), ((), ())), preferred_element_type=jnp.float32
         )
         out_v[r] = (gate_v[r] * linear).astype(jnp.bfloat16)
-    wait_all(recv1, 0)
-    wait_all(recv2, 2)
+    wait_blocks(recv_r, r_sems.at[0], n - 1)
+    wait_blocks(recv_l, l_sems.at[0], half - 1)
+    wait_blocks(recv_t, t_sems.at[0], half - 1)
 
 
 def fused(n, pair, pair_mask, ln_gain, ln_bias, w_proj, w_gate, tri_gain, tri_bias, w_out):
@@ -197,15 +208,17 @@
             pltpu.VMEM(w_proj.shape, bf16),
             pltpu.VMEM(w_gate.shape, bf16),
             pltpu.VMEM(w_out.shape, bf16),
-            pltpu.VMEM((n // 2, 2, 2, 16, k), bf16),
-            pltpu.VMEM((n, 2, 16, k), bf16),
-            pltpu.VMEM((n // 2, 2, 16, k), bf16),
-            pltpu.VMEM((n, 16, k), bf16),
-            pltpu.VMEM((2, n * 16, k), f32),
+            *[
+                pltpu.VMEM((blocks, rows * OWNED, k), bf16)
+                for blocks in (n // 2, n, n // 2, n // 2, n // 2, n // 2)
+            ],
+            pltpu.VMEM((n * rows * OWNED, k), f32),
             pltpu.VMEM((rows, k, c), f32),
             pltpu.VMEM((2, hidden, k), f32),
             pltpu.SemaphoreType.DMA((9,)),
-            pltpu.SemaphoreType.DMA((4,)),
+            pltpu.SemaphoreType.DMA((2,)),
+            pltpu.SemaphoreType.DMA((2,)),
+            pltpu.SemaphoreType.DMA((2,)),
         ],
         compiler_params=pltpu.CompilerParams(
             collective_id=0, has_side_effects=True, vmem_limit_bytes=16 * 2**20
@@ -216,14 +229,16 @@
 def fits(mesh, pair, w_out):
     n = mesh.shape["dap"]
     rows, k, c = pair.shape
+    hidden = w_out.shape[0]
     return (
         mesh.shape["sub"] == 1
-        and n % 4 == 0
-        and rows == GROUP
-        and w_out.shape[0] == GROUP * n
+        and n % 2 == 0
+        and 2 * hidden == OWNED * n
+        and rows * OWNED % 16 == 0
         and k == rows * n
-        and c == k
         and k % 128 == 0
+        and c == hidden
+        and c % 128 == 0
     )
 
 

time: 21.4 us -> 20.6 us (0.963)
  Pallas kernels: 20.6 us -> 19.8 us
    pallas_call x1, Pallas kernels: 20.6 us -> 19.8 us  [fused(): pl.pallas_call(run, out_shape=jax.ShapeDtypeStruct((rows, k, c), bf16), i...]
where the time goes in v3:
time: 20.6 us; the launch traced here: 20.5 us
  Pallas kernels  19.8 us (96%)
  local copies, waits for them, and re-layouts  0.66 us (3%)
    pallas_call x1, Pallas kernels, fused(): pl.pallas_call(run, out_shape=jax.ShapeDtypeStruct((rows, k, c), bf16), i...  19.8 us
    unnamed x1, local copies, waits for them, and re-layouts  0.66 us

profile of v3, /device:TPU:0, one launch (start us, length us, event | category | flops | bytes accessed | tf_op | source)
XLA Modules:
  0.0 20.5 jit_solution(5384461631590852460)
XLA Ops:
  0.0 19.8 %shard_map.91 = bf16[4,128,128]{2,1,0:T(8,128)(2,1)S(1)} custom-call(bf16[4,128,128]{2,1,0:T(8,128)(2,1)} %pair_r.1, s32[4,128]{1,0:T(4,128)} %mask_r.1, f32[1,128]{1,0:T(1,128)} %bitcast.4, f32[1,128]{1,0:T(1,128)} %bitcast.5, f32[1,128]{1,0:T(1,128)} %bitcast.6, f32[1,128]{1,0:T(1,128)} %bitcast.7, bf16[128,512]{1,0:T(8,128)(2,1)} %wp.1, ...), custom_call_target="tpu_custom_call" | custom-call | tf_op jit(solution)/shard_map/pallas_call | solution.py:199
  19.8 0.7 %copy.11 = bf16[4,128,128]{2,1,0:T(8,128)(2,1)} copy(bf16[4,128,128]{2,1,0:T(8,128)(2,1)S(1)} %shard_map.91) | data formatting | bytes 262144

commit v4 on v3

--- a/solution.py
+++ b/solution.py
@@ -138,9 +138,9 @@
     send_r[...] = jnp.concatenate(rights, axis=1).astype(jnp.bfloat16)
     send_l[...] = jnp.concatenate(lefts, axis=1).astype(jnp.bfloat16)
     pl.semaphore_wait(barrier, n - 1)
+    each_own(sender(send_l, recv_l, place, l_sems))
+    each_own(sender(send_r, recv_r, me, r_sems))
     each_other(sender(send_r, recv_r, me, r_sems))
-    each_own(sender(send_r, recv_r, me, r_sems))
-    each_own(sender(send_l, recv_l, place, l_sems))
     recv_r[me] = send_r[place]
     recv_l[place] = send_l[place]
 

time: 20.6 us -> 20 us (0.971)
  Pallas kernels: 19.8 us -> 19.2 us
    pallas_call x1, Pallas kernels: 19.8 us -> 19.2 us  [fused(): pl.pallas_call(run, out_shape=jax.ShapeDtypeStruct((rows, k, c), bf16), i...]
where the time goes in v4:
time: 20 us; the launch traced here: 19.8 us
  Pallas kernels  19.2 us (96%)
  local copies, waits for them, and re-layouts  0.66 us (3%)
    pallas_call x1, Pallas kernels, fused(): pl.pallas_call(run, out_shape=jax.ShapeDtypeStruct((rows, k, c), bf16), i...  19.2 us
    unnamed x1, local copies, waits for them, and re-layouts  0.66 us

profile of v4, /device:TPU:0, one launch (start us, length us, event | category | flops | bytes accessed | tf_op | source)
XLA Modules:
  0.0 19.8 jit_solution(13710970080850663182)
XLA Ops:
  0.0 19.2 %shard_map.91 = bf16[4,128,128]{2,1,0:T(8,128)(2,1)S(1)} custom-call(bf16[4,128,128]{2,1,0:T(8,128)(2,1)} %pair_r.1, s32[4,128]{1,0:T(4,128)} %mask_r.1, f32[1,128]{1,0:T(1,128)} %bitcast.4, f32[1,128]{1,0:T(1,128)} %bitcast.5, f32[1,128]{1,0:T(1,128)} %bitcast.6, f32[1,128]{1,0:T(1,128)} %bitcast.7, bf16[128,512]{1,0:T(8,128)(2,1)} %wp.1, ...), custom_call_target="tpu_custom_call" | custom-call | tf_op jit(solution)/shard_map/pallas_call | solution.py:199
  19.2 0.7 %copy.11 = bf16[4,128,128]{2,1,0:T(8,128)(2,1)} copy(bf16[4,128,128]{2,1,0:T(8,128)(2,1)S(1)} %shard_map.91) | data formatting | bytes 262144

commit v5 on v4

--- a/solution.py
+++ b/solution.py
@@ -160,14 +160,23 @@
         lefts.append(area[pl.ds(c, ours, stride=OWNED), :].astype(jnp.bfloat16))
     wait_blocks(recv_r, r_sems.at[1], n - 1)
     stage[...] = recv_r[...].astype(jnp.float32).reshape(n * rows * OWNED, k)
-    products = []
-    for c in range(OWNED):
-        right = stage[pl.ds(c, n * rows, stride=OWNED), :].astype(jnp.bfloat16)
-        products.append(nt_dot(lefts[c], right))
-    for c in range(OWNED):
-        area[pl.ds(c, ours, stride=OWNED), :] = products[c]
-    send_t[...] = area[...].astype(jnp.bfloat16).reshape(half, rows * OWNED, k)
-    each_own(sender(send_t, recv_t, place, t_sems))
+    rights = [stage[pl.ds(c, n * rows, stride=OWNED), :].astype(jnp.bfloat16) for c in range(OWNED)]
+    for part in range(2):
+        few, first = ours // 2, part * (half // 2)
+        for c in range(OWNED):
+            area[pl.ds(part * few * OWNED + c, few, stride=OWNED), :] = nt_dot(lefts[c][part * few : (part + 1) * few], rights[c])
+        send_t[pl.ds(first, half // 2)] = (
+            area[pl.ds(part * few * OWNED, few * OWNED), :].astype(jnp.bfloat16).reshape(half // 2, rows * OWNED, k)
+        )
+
+        @pl.loop(0, half // 2)
+        def _(s):
+            to = first + lax.rem(place + s, half // 2)
+
+            @pl.when(to != place)
+            def _():
+                sender(send_t, recv_t, place, t_sems)(base + to, to)
+
     recv_t[place] = send_t[place]
 
     wait_blocks(recv_t, t_sems.at[1], half - 1)
@@ -232,7 +241,7 @@
     hidden = w_out.shape[0]
     return (
         mesh.shape["sub"] == 1
-        and n % 2 == 0
+        and n % 4 == 0
         and 2 * hidden == OWNED * n
         and rows * OWNED % 16 == 0
         and k == rows * n

time: 20 us -> 19.8 us (0.990)
  no operation moved by 1% of the time
where the time goes in v5:
time: 19.8 us; the launch traced here: 19.7 us
  Pallas kernels  19 us (96%)
  local copies, waits for them, and re-layouts  0.66 us (3%)
    pallas_call x1, Pallas kernels, fused(): pl.pallas_call(run, out_shape=jax.ShapeDtypeStruct((rows, k, c), bf16), i...  19 us
    unnamed x1, local copies, waits for them, and re-layouts  0.66 us

profile of v5, /device:TPU:0, one launch (start us, length us, event | category | flops | bytes accessed | tf_op | source)
XLA Modules:
  0.0 19.7 jit_solution(16436289952875930496)
XLA Ops:
  0.0 19.0 %shard_map.91 = bf16[4,128,128]{2,1,0:T(8,128)(2,1)S(1)} custom-call(bf16[4,128,128]{2,1,0:T(8,128)(2,1)} %pair_r.1, s32[4,128]{1,0:T(4,128)} %mask_r.1, f32[1,128]{1,0:T(1,128)} %bitcast.4, f32[1,128]{1,0:T(1,128)} %bitcast.5, f32[1,128]{1,0:T(1,128)} %bitcast.6, f32[1,128]{1,0:T(1,128)} %bitcast.7, bf16[128,512]{1,0:T(8,128)(2,1)} %wp.1, ...), custom_call_target="tpu_custom_call" | custom-call | tf_op jit(solution)/shard_map/pallas_call | solution.py:208
  19.0 0.7 %copy.11 = bf16[4,128,128]{2,1,0:T(8,128)(2,1)} copy(bf16[4,128,128]{2,1,0:T(8,128)(2,1)S(1)} %shard_map.91) | data formatting | bytes 262144

commit v6 on v5

--- a/solution.py
+++ b/solution.py
@@ -58,8 +58,8 @@
 def kernel(
     n, pair_hbm, mask_hbm, vec_refs, w_proj_hbm, w_gate_hbm, w_out_hbm, out_v,
     pair_v, mask_v, vec_v, w_proj_v, w_gate_v, w_out_v,
-    send_r, recv_r, send_l, recv_l, send_t, recv_t, stage, gate_v, col_v,
-    in_sems, r_sems, l_sems, t_sems,
+    send_e, recv_o, recv_x, send_t, recv_t, stage, gate_v, col_v,
+    in_sems, o_sems, x_sems, t_sems,
 ):
     me = lax.axis_index("dap")
     rows, k, hidden = pair_v.shape[0], pair_v.shape[1], w_out_v.shape[0]
@@ -96,11 +96,11 @@
     gate_in = load(w_gate_hbm, w_gate_v, 3)
     out_in = load(w_out_hbm, w_out_v, 4)
 
-    def sender(send, recv, slot, sems):
+    def sender(send, recv, sems):
         def act(to, to_place):
             pltpu.make_async_remote_copy(
                 src_ref=send.at[to_place],
-                dst_ref=recv.at[slot],
+                dst_ref=recv.at[place],
                 send_sem=sems.at[0],
                 recv_sem=sems.at[1],
                 device_id={"dap": to},
@@ -135,14 +135,12 @@
         mask = mask_v[r : r + 1, :].astype(jnp.float32)
         lefts.append(edge(proj[0 : 2 * hidden], mask).reshape(half, OWNED, k))
         rights.append(edge(proj[2 * hidden : 4 * hidden], mask).reshape(half, OWNED, k))
-    send_r[...] = jnp.concatenate(rights, axis=1).astype(jnp.bfloat16)
-    send_l[...] = jnp.concatenate(lefts, axis=1).astype(jnp.bfloat16)
+    send_e[:, 0] = jnp.concatenate(rights, axis=1).astype(jnp.bfloat16)
+    send_e[:, 1] = jnp.concatenate(lefts, axis=1).astype(jnp.bfloat16)
     pl.semaphore_wait(barrier, n - 1)
-    each_own(sender(send_l, recv_l, place, l_sems))
-    each_own(sender(send_r, recv_r, me, r_sems))
-    each_other(sender(send_r, recv_r, me, r_sems))
-    recv_r[me] = send_r[place]
-    recv_l[place] = send_l[place]
+    each_own(sender(send_e, recv_o, o_sems))
+    each_other(sender(send_e.at[:, 0], recv_x, x_sems))
+    recv_o[place] = send_e[place]
 
     gate_in.wait()
     for r in range(rows):
@@ -152,30 +150,34 @@
     out_in.wait()
 
     ours = half * rows
-    wait_blocks(recv_l, l_sems.at[1], half - 1)
-    lefts = []
-    area = stage.at[pl.ds(0, ours * OWNED)]
-    area[...] = recv_l[...].astype(jnp.float32).reshape(ours * OWNED, k)
-    for c in range(OWNED):
-        lefts.append(area[pl.ds(c, ours, stride=OWNED), :].astype(jnp.bfloat16))
-    wait_blocks(recv_r, r_sems.at[1], n - 1)
-    stage[...] = recv_r[...].astype(jnp.float32).reshape(n * rows * OWNED, k)
+    size = ours * OWNED
+
+    def spread(start, blocks):
+        stage[pl.ds(pl.multiple_of(start * rows * OWNED, size), size)] = blocks.astype(jnp.float32).reshape(size, k)
+
+    wait_blocks(recv_o, o_sems.at[1], half - 1)
+    spread(0, recv_o[:, 1])
+    area = stage.at[pl.ds(0, size)]
+    lefts = [area[pl.ds(c, ours, stride=OWNED), :].astype(jnp.bfloat16) for c in range(OWNED)]
+    spread(base, recv_o[:, 0])
+    wait_blocks(recv_x, x_sems.at[1], half)
+    spread(half - base, recv_x[...])
     rights = [stage[pl.ds(c, n * rows, stride=OWNED), :].astype(jnp.bfloat16) for c in range(OWNED)]
+    few = half // 2
     for part in range(2):
-        few, first = ours // 2, part * (half // 2)
+        span = few * rows
+        cut = stage.at[pl.ds(part * span * OWNED, span * OWNED)]
         for c in range(OWNED):
-            area[pl.ds(part * few * OWNED + c, few, stride=OWNED), :] = nt_dot(lefts[c][part * few : (part + 1) * few], rights[c])
-        send_t[pl.ds(first, half // 2)] = (
-            area[pl.ds(part * few * OWNED, few * OWNED), :].astype(jnp.bfloat16).reshape(half // 2, rows * OWNED, k)
-        )
-
-        @pl.loop(0, half // 2)
+            cut[pl.ds(c, span, stride=OWNED), :] = nt_dot(lefts[c][part * span : (part + 1) * span], rights[c])
+        send_t[pl.ds(part * few, few)] = cut[...].astype(jnp.bfloat16).reshape(few, rows * OWNED, k)
+
+        @pl.loop(0, few)
         def _(s):
-            to = first + lax.rem(place + s, half // 2)
+            to = part * few + lax.rem(place + s, few)
 
             @pl.when(to != place)
             def _():
-                sender(send_t, recv_t, place, t_sems)(base + to, to)
+                sender(send_t, recv_t, t_sems)(base + to, to)
 
     recv_t[place] = send_t[place]
 
@@ -190,8 +192,8 @@
             normed, w_out_v[...], (((0,), (0,)), ((), ())), preferred_element_type=jnp.float32
         )
         out_v[r] = (gate_v[r] * linear).astype(jnp.bfloat16)
-    wait_blocks(recv_r, r_sems.at[0], n - 1)
-    wait_blocks(recv_l, l_sems.at[0], half - 1)
+    wait_blocks(recv_o, o_sems.at[0], half - 1)
+    wait_blocks(recv_x, x_sems.at[0], half)
     wait_blocks(recv_t, t_sems.at[0], half - 1)
 
 
@@ -218,8 +220,8 @@
             pltpu.VMEM(w_gate.shape, bf16),
             pltpu.VMEM(w_out.shape, bf16),
             *[
-                pltpu.VMEM((blocks, rows * OWNED, k), bf16)
-                for blocks in (n // 2, n, n // 2, n // 2, n // 2, n // 2)
+                pltpu.VMEM((n // 2, *sides, rows * OWNED, k), bf16)
+                for sides in ((2,), (2,), (), (), ())
             ],
             pltpu.VMEM((n * rows * OWNED, k), f32),
             pltpu.VMEM((rows, k, c), f32),

time: 19.8 us -> 19.8 us (level)
  no operation moved by 1% of the time
where the time goes in v6:
time: 19.8 us; the launch traced here: 19.6 us
  Pallas kernels  19 us (96%)
  local copies, waits for them, and re-layouts  0.66 us (3%)
    pallas_call x1, Pallas kernels, fused(): pl.pallas_call(run, out_shape=jax.ShapeDtypeStruct((rows, k, c), bf16), i...  19 us
    unnamed x1, local copies, waits for them, and re-layouts  0.66 us

profile of v6, /device:TPU:0, one launch (start us, length us, event | category | flops | bytes accessed | tf_op | source)
XLA Modules:
  0.0 19.6 jit_solution(15851026380135704147)
XLA Ops:
  0.0 19.0 %shard_map.91 = bf16[4,128,128]{2,1,0:T(8,128)(2,1)S(1)} custom-call(bf16[4,128,128]{2,1,0:T(8,128)(2,1)} %pair_r.1, s32[4,128]{1,0:T(4,128)} %mask_r.1, f32[1,128]{1,0:T(1,128)} %bitcast.4, f32[1,128]{1,0:T(1,128)} %bitcast.5, f32[1,128]{1,0:T(1,128)} %bitcast.6, f32[1,128]{1,0:T(1,128)} %bitcast.7, bf16[128,512]{1,0:T(8,128)(2,1)} %wp.1, ...), custom_call_target="tpu_custom_call" | custom-call | tf_op jit(solution)/shard_map/pallas_call | solution.py:210
  19.0 0.7 %copy.11 = bf16[4,128,128]{2,1,0:T(8,128)(2,1)} copy(bf16[4,128,128]{2,1,0:T(8,128)(2,1)S(1)} %shard_map.91) | data formatting | bytes 262144
